TPU v7x, 512 devices: a whole 4x4x16 slice. The times are simulated.
512 devices in a mesh: blk: 64 (over x_lo, z, core), tp: 8 (over x_hi, y).
Axes of the slice: x: 4 (x_hi: 2, x_lo: 2; x = x_hi * 2 + x_lo), y: 4, z: 16, core: 2. Of those that a mesh axis runs over, the one named last changes fastest.
Arguments:
- tokens: bfloat16 [32768, 8192], P('blk', 'tp'), may hold values from -40 to 40
- gain: float32 [8192], P('tp'), may hold values from 0.1 to 1.9
- w_value: bfloat16 [8192, 1024], P(('tp', 'blk')), may hold values from -0.0625 to 0.0625
- cotangent: bfloat16 [32768, 1024], P('blk'), may hold values from -6 to 6
Outputs:
- values: bfloat16 [32768, 1024], P('blk')
- grad_weight: float32 [8192, 1024], P(('tp', 'blk'))
- grad_tokens: bfloat16 [32768, 8192], P('blk', 'tp')
All inputs are finite; a program needn't handle non-finite values.
Results may differ from a plain program's by a relative error of at most 0.0049.
Values may be sent and summed in bfloat16 or wider, within the bound.
A program may use at most 64 MiB of HBM per device.

v0:
```python
import jax
import jax.numpy as jnp
from jax import lax
from jax.sharding import PartitionSpec as P

D = 8192


EPS = 1e-05


def on_device(tokens, gain, w_value, cotangent):
    xf = tokens.astype(jnp.float32)
    squares = lax.psum(jnp.sum(xf * xf, axis=1), "tp")
    scale = lax.rsqrt(squares / D + EPS)
    normed = (xf * scale[:, None] * gain[None, :]).astype(jnp.bfloat16)
    gathered = lax.all_gather(w_value, "blk", axis=0, tiled=True)
    partial_value = jnp.dot(normed, gathered, preferred_element_type=jnp.float32)
    grad_normed = lax.dot_general(
        cotangent, gathered, (((1,), (1,)), ((), ())), preferred_element_type=jnp.float32
    )
    values = lax.psum(partial_value, "tp").astype(jnp.bfloat16)
    term = lax.dot_general(
        normed, cotangent, (((0,), (0,)), ((), ())), preferred_element_type=jnp.float32
    )
    grad_weight = lax.psum_scatter(term, "blk", scatter_dimension=0, tiled=True)
    inner = lax.psum(jnp.sum(gain[None, :] * grad_normed * xf, axis=1), "tp")
    grad_tokens = (
        scale[:, None] * gain[None, :] * grad_normed - xf * (scale**3 * inner / D)[:, None]
    )
    return (values, grad_weight, grad_tokens.astype(jnp.bfloat16))


def solution(mesh):
    return jax.shard_map(
        on_device,
        mesh=mesh,
        in_specs=(P("blk", "tp"), P("tp"), P(("tp", "blk"), None), P("blk", None)),
        out_specs=(P("blk", None), P(("tp", "blk"), None), P("blk", "tp")),
        check_vma=False,
    )
```

profile of v0, /device:TPU:6, one launch (start us, length us, event | category | flops | bytes accessed | tf_op | source)
XLA Modules:
  0.0 400.2 jit_solution(6936487684446704884)
XLA Ops:
  7.2 0.0 copy-start
  7.2 0.0 all-gather.2.cloned.1.call-start
  7.2 0.7 all-gather.2.cloned.1.call-update
  7.9 0.0 copy-start.1
  7.9 0.0 copy-start.2
  7.9 0.0 reduce-scatter.2.cloned.1.call-start
  8.0 128.5 %all-gather.2.cloned.1.call-done = bf16[1024,1024]{1,0:T(8,128)(2,1)} async-done(((bf16[16,1024]{1,0:T(8,128)(2,1)}), bf16[1024,1024]{1,0:T(8,128)(2,1)}) %all-gather.2.cloned.1.call-update) | async-done | bytes 2097168 | tf_op jit(solution)/shard_map/all_gather | solution.py:17
  136.4 0.0 copy-done
  136.4 4.6 %fusion.3 = (f32[512]{0:T(512)S(1)}, f32[512]{0:T(512)S(1)}, f32[512,1024]{1,0:T(8,128)}) fusion(bf16[512,1024]{1,0:T(8,128)(2,1)} %param.4, f32[1024]{0:T(1024)} %param.5, bf16[512,1024]{1,0:T(8,128)(2,1)S(1)} %copy-done, bf16[1024,1024]{1,0:T(8,128)(2,1)} %all-gather.2.cloned.1.call-done), kind=kOutput, calls=%fused_computation.7 | convolution fusion | flops 1076886528 | bytes 6299648 | tf_op jit(solution)/shard_map/dot_general | solution.py:19
  141.0 22.5 %psum.21 = f32[512]{0:T(512)S(1)} all-reduce(f32[512]{0:T(512)S(1)} %get-tuple-element.4), channel_id=1, replica_groups=mesh['blk'=64,'tp'=8] {'tp'}, use_global_device_ids=true, to_apply=%region_1.0 | all-reduce | flops 512 | bytes 4096 | tf_op jit(solution)/shard_map/psum | solution.py:14
  163.5 0.0 copy-done.1
  163.5 0.0 copy-done.2
  163.5 3.3 fusion.6
  166.8 0.0 reduce-scatter.2.cloned.1.call-update
  166.9 4.3 %fusion.8 = f32[512,1024]{1,0:T(8,128)} fusion(bf16[1024,1024]{1,0:T(8,128)(2,1)} %all-gather.2.cloned.1.call-done, bf16[512,1024]{1,0:T(8,128)(2,1)S(1)} %copy-done.1, f32[1024]{0:T(1024)S(1)} %copy-done.2, f32[512]{0:T(512)S(1)} %add_rsqrt_fusion), kind=kOutput, calls=%fused_computation.11 | convolution fusion | flops 1075838976 | bytes 5249024 | tf_op jit(solution)/shard_map/dot_general | solution.py:18
  171.2 84.1 %all-reduce.2 = (bf16[512,1024]{1,0:T(8,128)(2,1)}, f32[512]{0:T(512)S(1)}) all-reduce(f32[512,1024]{1,0:T(8,128)} %fusion.8, f32[512]{0:T(512)S(1)} %get-tuple-element.3), channel_id=1, replica_groups=mesh['blk'=64,'tp'=8] {'tp'}, use_global_device_ids=true, to_apply=%region_2.0 | all-reduce | flops 524800 | bytes 3149824 | tf_op jit(solution)/shard_map/psum | solution.py:22
  255.3 3.0 fusion.5
  258.3 135.1 %reduce-scatter.2.cloned.1.call-done = f32[16,1024]{1,0:T(8,128)} async-done(((f32[1024,1024]{1,0:T(8,128)}), f32[16,1024]{1,0:T(8,128)}) %reduce-scatter.2.cloned.1.call-update) | async-done | bytes 65552 | tf_op jit(solution)/shard_map/reduce_scatter | solution.py:26
  (2 shorter events, 0.0 us)
Async XLA Ops:
  7.2 129.3 %copy-start = (bf16[512,1024]{1,0:T(8,128)(2,1)S(1)}, bf16[512,1024]{1,0:T(8,128)(2,1)}, u32[]{:S(2)}) copy-start(bf16[512,1024]{1,0:T(8,128)(2,1)} %param.7) | copy-start | bytes 3145732
  7.2 129.3 %all-gather.2.cloned.1.call-start = ((), (), s32[]{:S(2)}) async-start(), calls=%async_computation.1 | async-start | bytes 2129920 | tf_op jit(solution)/shard_map/all_gather | solution.py:17
  7.9 155.6 %copy-start.1 = (bf16[512,1024]{1,0:T(8,128)(2,1)S(1)}, bf16[512,1024]{1,0:T(8,128)(2,1)}, u32[]{:S(2)}) copy-start(bf16[512,1024]{1,0:T(8,128)(2,1)} %param.4) | copy-start | bytes 3145732
  7.9 155.6 %copy-start.2 = (f32[1024]{0:T(1024)S(1)}, f32[1024]{0:T(1024)}, u32[]{:S(2)}) copy-start(f32[1024]{0:T(1024)} %param.5) | copy-start | bytes 12292
  7.9 385.4 %reduce-scatter.2.cloned.1.call-start = ((), (), s32[]{:S(2)}) async-start(), calls=%async_computation.2 | async-start | bytes 4259840 | tf_op jit(solution)/shard_map/reduce_scatter | solution.py:26
Sparse Core Ops, SparseCore 0:
  10.2 126.2 all-gather.1
  167.0 226.3 reduce-scatter.1
where the time goes:
time: 402 us; the launch traced here: 400 us
  waiting for transfers between devices  264 us (66%)
  blocking collectives  107 us (27%)
  between operations  14.1 us (4%)
  matrix products  12.2 us (3%)
    reduce_scatter x1, waiting for transfers between devices, on_device(): grad_weight = lax.psum_scatter(term, 'blk', scatter_dimension=0, tiled=True)  135 us
    all_gather x1, waiting for transfers between devices, on_device(): gathered = lax.all_gather(w_value, 'blk', axis=0, tiled=True)  128 us
    psum x1, blocking collectives, on_device(): values = lax.psum(partial_value, 'tp').astype(jnp.bfloat16)  84.1 us
    psum x1, blocking collectives, on_device(): squares = lax.psum(jnp.sum(xf * xf, axis=1), 'tp')  22.5 us
  transfers between devices with their start and end apart: 2, of which 2 were waited for; matrix products, arithmetic and copies ran while one was open for 2% of the time, Pallas kernels for 0%

commit v1 on v0

v1 whole, which is shorter than its diff:
```python
import functools

import jax
import jax.numpy as jnp
from jax import lax
from jax.experimental import pallas as pl
from jax.experimental.pallas import tpu as pltpu
from jax.sharding import PartitionSpec as P

D = 8192
EPS = 1e-05
MESH = pl.DeviceIdType.MESH
F32 = jnp.float32
BF16 = jnp.bfloat16

NZ = 16
NT = 8
ROWS = 512
FEAT = 1024
KV = 1024
OWN = ROWS // NT
NJ = 4
CW = KV // NJ


def kernel(
    x_ref, gain_ref, w_ref, cot_ref,
    val_ref, gw_ref, gt_ref,
    w_all, normed, scale_b, sq_mine, sq_all,
    pv, rv, own_val, gs, s_acc,
    tf, tb, tr, t2, xs, xr, gsend, leaf, chain,
    wz_s, wz_r, wd_s, wd_r, wx_s, wx_r, wf_s, wf_r, sib_s, sib_r,
    sq_s, sq_r, rs_s, rs_r, ag_s, ag_r,
    core_s, core_r, xs_s, xs_r, leaf_s, leaf_r, chain_s, chain_r,
):
    blk = lax.axis_index("blk")
    tp = lax.axis_index("tp")
    xlo = blk // (2 * NZ)
    z = (blk // 2) % NZ
    core = blk % 2
    sign = (1 - 2 * core, 2 * core - 1)

    def at_z(step, other_x=False):
        x = 1 - xlo if other_x else xlo
        return (x * (2 * NZ) + ((z + step + 2 * NZ) % NZ) * 2 + core, tp)

    sibling = (xlo * (2 * NZ) + z * 2 + 1 - core, tp)
    partner = (blk, tp)

    def tp_peer(k):
        return (blk, (tp + k) % NT)

    def copy(src, dst, s, r, dev):
        return pltpu.make_async_remote_copy(
            src_ref=src, dst_ref=dst, send_sem=s, recv_sem=r, device_id=dev, device_id_type=MESH
        )

    barrier = pltpu.get_barrier_semaphore()
    peers = [at_z(0, True), sibling]
    for step in (1, 2, -1, -2):
        peers += [at_z(step), at_z(step, True)]
    peers += [tp_peer(k) for k in range(1, NT)]
    for dev in peers:
        pl.semaphore_signal(barrier, inc=1, device_id=dev, device_id_type=MESH)

    for q in range(ROWS // 128):
        rows = pl.ds(q * 128, 128)
        acc = jnp.zeros((128, 128), F32)
        for n in range(FEAT // 128):
            xf = x_ref[rows, n * 128 : (n + 1) * 128].astype(F32)
            acc += xf * xf
        sq_mine[:, rows] = jnp.sum(acc.T, axis=0, keepdims=True)
    w_all[xlo, z, core] = w_ref[...]
    pl.semaphore_wait(barrier, len(peers))

    def w_origin(i, k):
        return (z - sign[i] * k + 2 * NZ) % NZ

    mine = w_all.at[xlo, z, core]
    first = []
    for k in (2, 1):
        for i in range(2):
            first.append(copy(mine, mine, wz_s.at[i, k], wz_r.at[i, k], at_z(sign[i] * k)))
            first.append(copy(mine, mine, wd_s.at[i, k], wd_r.at[i, k], at_z(sign[i] * k, True)))
    first.append(copy(mine, mine, wx_s, wx_r, at_z(0, True)))
    for c in first:
        c.start()

    def sq_copy(k):
        return copy(sq_mine, sq_all.at[tp], sq_s.at[k], sq_r.at[NT - k], tp_peer(k))

    def sq_recv(k):
        src = (tp + k) % NT
        return copy(sq_mine, sq_all.at[src], sq_s.at[k], sq_r.at[k], tp_peer(k))

    for k in range(1, NT):
        sq_copy(k).start()
    sq_all[tp] = sq_mine[...]

    def w_forward(i, m, far):
        pair = w_all.at[:, w_origin(i, 2 * m), core]
        k = 2 * m + 1 + far
        return copy(pair, pair, wf_s.at[i, k], wz_r.at[i, k], at_z(sign[i] * (1 + far)))

    def w_wait(i, k):
        if k <= 2:
            one = w_all.at[xlo, w_origin(i, k), core]
            two = w_all.at[1 - xlo, w_origin(i, k), core]
            copy(one, one, wz_s.at[i, k], wz_r.at[i, k], partner).wait_recv()
            copy(two, two, wd_s.at[i, k], wd_r.at[i, k], partner).wait_recv()
        else:
            pair = w_all.at[:, w_origin(i, k), core]
            copy(pair, pair, wf_s.at[i, k], wz_r.at[i, k], partner).wait_recv()

    def sib_copy(origin, slot):
        pair = w_all.at[:, origin, core]
        return copy(pair, pair, sib_s.at[slot], sib_r.at[slot], sibling)

    def sib_slot(i, k):
        return w_origin(i, k)

    def to_sibling(i, k):
        o = w_origin(i, k)
        sib_copy(o, o).start()

    forwards = []

    def w_step(m):
        for i in range(2):
            w_wait(i, 2 * m)
            if not (i == 1 and 2 * m + 2 > 6):
                c = w_forward(i, m, 1)
                c.start()
                forwards.append(c)
            c = w_forward(i, m, 0)
            c.start()
            forwards.append(c)
        for i in range(2):
            to_sibling(i, 2 * m)

    def w_leaf(k):
        for i in range(2):
            w_wait(i, k)
            to_sibling(i, k)

    w_step(1)
    other = w_all.at[1 - xlo, z, core]
    copy(other, other, wx_s, wx_r, partner).wait_recv()
    sib_copy(z, z).start()
    w_leaf(1)

    for k in range(1, NT):
        sq_recv(k).wait_recv()
    total = sq_all[0]
    for k in range(1, NT):
        total = total + sq_all[k]
    scale_row = lax.rsqrt(total / D + EPS)
    for q in range(ROWS // 128):
        rows = pl.ds(q * 128, 128)
        sb = jnp.broadcast_to(scale_row[:, q * 128 : (q + 1) * 128], (128, 128)).T
        scale_b[rows, :] = sb

    @pl.loop(0, ROWS // 128)
    def _(q):
        rows = pl.ds(pl.multiple_of(q * 128, 128), 128)
        sb = scale_b[rows, :][:, :1]
        normed[rows, :] = (x_ref[rows, :].astype(F32) * sb * gain_ref[...]).astype(BF16)

    w_step(2)

    for q in range(4):
        part = lax.dot_general(
            normed[:, q * 256 : (q + 1) * 256], cot_ref[...], (((0,), (0,)), ((), ())),
            preferred_element_type=F32,
        )
        tf[q // 2, (q % 2) * 8 : (q % 2) * 8 + 8] = part.reshape(8, 2, 16, KV)

    def core_copy():
        return copy(tb, tr, core_s, core_r, sibling)

    @pl.loop(0, NZ)
    def _(n):
        for h in range(2):
            tb[h, n] = tf[h, n, 1 - core].astype(BF16)

    core_copy().start()
    w_leaf(3)
    w_step(3)

    core_copy().wait_recv()

    def z_at(i, k):
        return (z - sign[i] * k + 2 * NZ) % NZ

    def x_copy(n):
        return copy(xs.at[n], xr.at[n], xs_s.at[n], xs_r.at[n], at_z(0, True))

    order = [(0, 8)] + [(i, k) for k in (7, 6, 5, 4, 3, 2, 1) for i in range(2)] + [(0, 0)]
    for i, k in order:
        n = z_at(i, k)
        xs[n] = (tf[1 - xlo, n, core] + tr[1 - xlo, n].astype(F32)).astype(BF16)
        x_copy(n).start()
    w_leaf(5)

    @pl.loop(0, NZ)
    def _(n):
        t2[n] = tf[xlo, n, core] + tr[xlo, n].astype(F32)

    w_leaf(7)
    w_wait(0, 8)
    to_sibling(0, 8)
    for o in range(NZ):
        pair = w_all.at[:, o, 1 - core]
        copy(pair, pair, sib_s.at[o], sib_r.at[o], sibling).wait_recv()

    def rs_copy(j, k):
        dst = (tp + k) % NT
        src = pv.at[pl.ds(pl.multiple_of(dst * OWN, OWN), OWN), pl.ds(j * CW, CW)]
        return copy(src, rv.at[j, tp], rs_s.at[j, k], rs_r.at[j, NT - k], tp_peer(k))

    def ag_copy(j, k):
        rows = pl.ds(pl.multiple_of(tp * OWN, OWN), OWN)
        dst = val_ref.at[rows, pl.ds(j * CW, CW)]
        return copy(own_val.at[j], dst, ag_s.at[j, k], ag_r.at[j, NT - k], tp_peer(k))

    def partial(j):
        cols = slice(j * CW, (j + 1) * CW)
        wc = w_all[:, :, :, :, cols].reshape(FEAT, CW)

        @pl.loop(0, 2)
        def _(h):
            rows = pl.ds(pl.multiple_of(h * 256, 256), 256)
            pv[rows, cols] = jnp.dot(
                normed[rows, :], wc, preferred_element_type=F32
            ).astype(BF16)

        for k in (1, 2, 3, 5, 6, 7, 4):
            rs_copy(j, k).start()
        rv[j, tp] = pv[pl.ds(pl.multiple_of(tp * OWN, OWN), OWN), cols]

    def reduce(j):
        for k in range(1, NT):
            src = (tp + k) % NT
            copy(rv.at[j, src], rv.at[j, src], rs_s.at[j, k], rs_r.at[j, k], partner).wait_recv()
        v = rv[j, 0].astype(F32)
        for k in range(1, NT):
            v += rv[j, k].astype(F32)
        own_val[j] = v.astype(BF16)
        for k in (1, 2, 3, 5, 6, 7, 4):
            ag_copy(j, k).start()
        val_ref[pl.ds(pl.multiple_of(tp * OWN, OWN), OWN), j * CW : (j + 1) * CW] = own_val[j]

    def gather(j):
        for k in range(1, NT):
            src = (tp + k) % NT
            rows = pl.ds(pl.multiple_of(src * OWN, OWN), OWN)
            dst = val_ref.at[rows, pl.ds(j * CW, CW)]
            copy(dst, dst, ag_s.at[j, k], ag_r.at[j, k], partner).wait_recv()
        cols = slice(j * CW, (j + 1) * CW)
        prod = val_ref[:, cols].astype(F32) * cot_ref[:, cols].astype(F32)
        s = prod[:, :128] + prod[:, 128:]
        if j == 0:
            s_acc[...] = s
        else:
            s_acc[...] += s

    def x_sum(i, k):
        n = z_at(i, k)
        copy(xs.at[n], xr.at[n], xs_s.at[n], xs_r.at[n], partner).wait_recv()
        return t2[n] + xr[n].astype(F32)

    def leaf_copy(i, m):
        return copy(gsend.at[i, 2 * m + 1], leaf.at[i, m], leaf_s.at[i, m], leaf_r.at[i, m], at_z(-sign[i]))

    def chain_copy(i, m):
        return copy(
            gsend.at[i, 2 * m + 2], chain.at[i, m], chain_s.at[i, m], chain_r.at[i, m], at_z(-2 * sign[i])
        )

    def g_leaf(k):
        for i in range(2):
            gsend[i, k] = x_sum(i, k).astype(BF16)
            leaf_copy(i, (k - 1) // 2).start()

    def g_chain(k):
        for i in range(2):
            if k == 8 and i == 1:
                continue
            acc = x_sum(i, k)
            if k < 8:
                m = k // 2
                leaf_copy(i, m).wait_recv()
                acc += leaf[i, m].astype(F32)
                if not (i == 1 and m == 3):
                    chain_copy(i, m).wait_recv()
                    acc += chain[i, m].astype(F32)
            gsend[i, k] = acc.astype(BF16)
            chain_copy(i, k // 2 - 1).start()

    def g_last():
        acc = x_sum(0, 0)
        for i in range(2):
            leaf_copy(i, 0).wait_recv()
            chain_copy(i, 0).wait_recv()
            acc += leaf[i, 0].astype(F32) + chain[i, 0].astype(F32)
        gw_ref[...] = acc

    def grad(q):
        cols = slice(q * 256, (q + 1) * 256)
        wq = w_all[q // 2, (q % 2) * 8 : (q % 2) * 8 + 8].reshape(256, KV)

        @pl.loop(0, 2)
        def _(h):
            rows = pl.ds(pl.multiple_of(h * 256, 256), 256)
            gn = lax.dot_general(
                cot_ref[rows, :], wq, (((1,), (1,)), ((), ())), preferred_element_type=F32
            )
            gs[rows, cols] = scale_b[rows, :][:, :1] * gain_ref[:, cols] * gn

    partial(0)
    partial(1)
    g_chain(8)
    g_leaf(7)
    partial(2)
    partial(3)
    g_leaf(5)
    grad(0)
    g_chain(6)
    reduce(0)
    g_leaf(3)
    g_leaf(1)
    grad(1)
    reduce(1)
    g_chain(4)
    grad(2)
    reduce(2)
    g_chain(2)
    grad(3)
    reduce(3)
    gather(0)
    gather(1)
    g_last()
    gather(2)
    gather(3)

    @pl.loop(0, ROWS // 128)
    def _(q):
        rows = pl.ds(pl.multiple_of(q * 128, 128), 128)
        sb = scale_b[rows, :][:, :1]
        inner = jnp.sum(s_acc[rows, :], axis=1, keepdims=True)
        coef = sb * sb * inner / D
        gt_ref[rows, :] = (gs[rows, :] - x_ref[rows, :].astype(F32) * coef).astype(BF16)

    for c in first + forwards:
        c.wait_send()
    for o in range(NZ):
        sib_copy(o, o).wait_send()
    for k in range(1, NT):
        sq_copy(k).wait_send()
    core_copy().wait_send()
    for n in range(NZ):
        x_copy(n).wait_send()
    for j in range(NJ):
        for k in range(1, NT):
            rs_copy(j, k).wait_send()
            ag_copy(j, k).wait_send()
    for i in range(2):
        for m in range(4):
            leaf_copy(i, m).wait_send()
            if not (i == 1 and m == 3):
                chain_copy(i, m).wait_send()


def on_device(tokens, gain, w_value, cotangent):
    vmem = pl.BlockSpec(memory_space=pltpu.VMEM)
    dma = pltpu.SemaphoreType.DMA
    scratch = [
        pltpu.VMEM((2, NZ, 2, 16, KV), BF16),
        pltpu.VMEM((ROWS, FEAT), BF16),
        pltpu.VMEM((ROWS, 128), F32),
        pltpu.VMEM((1, ROWS), F32),
        pltpu.VMEM((NT, 1, ROWS), F32),
        pltpu.VMEM((ROWS, KV), BF16),
        pltpu.VMEM((NJ, NT, OWN, CW), BF16),
        pltpu.VMEM((NJ, OWN, CW), BF16),
        pltpu.VMEM((ROWS, FEAT), F32),
        pltpu.VMEM((ROWS, 128), F32),
        pltpu.VMEM((2, NZ, 2, 16, KV), F32),
        pltpu.VMEM((2, NZ, 16, KV), BF16),
        pltpu.VMEM((2, NZ, 16, KV), BF16),
        pltpu.VMEM((NZ, 16, KV), F32),
        pltpu.VMEM((NZ, 16, KV), BF16),
        pltpu.VMEM((NZ, 16, KV), BF16),
        pltpu.VMEM((2, 9, 16, KV), BF16),
        pltpu.VMEM((2, 4, 16, KV), BF16),
        pltpu.VMEM((2, 4, 16, KV), BF16),
        dma((2, 9)), dma((2, 9)),
        dma((2, 3)), dma((2, 3)),
        dma, dma,
        dma((2, 9)), dma((2, 9)),
        dma((NZ,)), dma((NZ,)),
        dma((NT,)), dma((NT,)),
        dma((NJ, NT)), dma((NJ, NT)),
        dma((NJ, NT)), dma((NJ, NT)),
        dma, dma,
        dma((NZ,)), dma((NZ,)),
        dma((2, 4)), dma((2, 4)),
        dma((2, 4)), dma((2, 4)),
    ]
    return pl.pallas_call(
        kernel,
        name="value_projection",
        out_shape=(
            jax.ShapeDtypeStruct((ROWS, KV), BF16),
            jax.ShapeDtypeStruct((16, KV), F32),
            jax.ShapeDtypeStruct((ROWS, FEAT), BF16),
        ),
        in_specs=[vmem] * 4,
        out_specs=(vmem,) * 3,
        scratch_shapes=scratch,
        cost_estimate=pl.CostEstimate(
            flops=6 * ROWS * FEAT * KV, bytes_accessed=8 * 2**20, transcendentals=ROWS
        ),
        compiler_params=pltpu.CompilerParams(
            collective_id=0, has_side_effects=True, vmem_limit_bytes=56 * 2**20
        ),
    )(tokens, gain.reshape(1, FEAT), w_value, cotangent)


def solution(mesh):
    return jax.shard_map(
        on_device,
        mesh=mesh,
        in_specs=(P("blk", "tp"), P("tp"), P(("tp", "blk"), None), P("blk", None)),
        out_specs=(P("blk", None), P(("tp", "blk"), None), P("blk", "tp")),
        check_vma=False,
    )
```

time: 402 us -> 76.7 us (0.19)
  the two profiles are of different devices: /device:TPU:6 before, /device:TPU:2 now
where the time goes in v1:
time: 76.7 us; the launch traced here: 76.5 us
  Pallas kernels  71.9 us (94%)
  local copies, waits for them, and re-layouts  3.96 us (5%)
    pallas_call x1, Pallas kernels, on_device(): pl.pallas_call(kernel, name='value_projection', out_shape=(jax.ShapeDtype...  71.9 us
    unnamed x7, local copies, waits for them, and re-layouts  3.96 us

profile of v1, /device:TPU:2, one launch (start us, length us, event | category | flops | bytes accessed | tf_op | source)
XLA Modules:
  0.0 76.5 jit_solution(6768289119886202442)
XLA Ops:
  0.6 71.9 %value_projection.1 = (bf16[512,1024]{1,0:T(8,128)(2,1)}, f32[16,1024]{1,0:T(8,128)}, bf16[512,1024]{1,0:T(8,128)(2,1)}) custom-call(bf16[512,1024]{1,0:T(8,128)(2,1)} %x_ref.1, f32[1,1024]{1,0:T(1,128)} %bitcast.1, bf16[16,1024]{1,0:T(8,128)(2,1)} %w_ref.1, bf16[512,1024]{1,0:T(8,128)(2,1)} %cot_ref.1), custom_call_target="tpu_custom_call" | custom-call | flops 3221225472 | bytes 8388608 | tf_op jit(solution)/shard_map/value_projection/pallas_call | solution.py:410
  72.5 0.0 copy-start.1
  72.5 0.0 copy-start
  72.5 2.4 %copy.10 = bf16[512,1024]{1,0:T(8,128)(2,1)} copy(bf16[512,1024]{1,0:T(8,128)(2,1)} %get-tuple-element.6) | data formatting | bytes 2097152
  74.9 0.0 copy-done.1
  74.9 0.6 copy.11
  75.5 0.0 copy-done
  75.5 1.0 %copy.12 = bf16[512,1024]{1,0:T(8,128)(2,1)} copy(bf16[512,1024]{1,0:T(8,128)(2,1)S(1)} %copy-done) | data formatting | bytes 2097152
Async XLA Ops:
  72.5 2.4 %copy-start.1 = (f32[16,1024]{1,0:T(8,128)S(1)}, f32[16,1024]{1,0:T(8,128)}, u32[]{:S(2)}) copy-start(f32[16,1024]{1,0:T(8,128)} %get-tuple-element.7) | copy-start | bytes 196612
  72.5 3.0 %copy-start = (bf16[512,1024]{1,0:T(8,128)(2,1)S(1)}, bf16[512,1024]{1,0:T(8,128)(2,1)}, u32[]{:S(2)}) copy-start(bf16[512,1024]{1,0:T(8,128)(2,1)} %get-tuple-element.8) | copy-start | bytes 3145732

commit v2 on v0

v2 whole, which is shorter than its diff:
```python
import functools

import jax
import jax.numpy as jnp
from jax import lax
from jax.experimental import pallas as pl
from jax.experimental.pallas import tpu as pltpu
from jax.sharding import PartitionSpec as P

D = 8192
EPS = 1e-05
MESH = pl.DeviceIdType.MESH
F32 = jnp.float32
BF16 = jnp.bfloat16

NZ = 16
NT = 8
ROWS = 512
FEAT = 1024
KV = 1024
OWN = ROWS // NT
NY = 4
NJ = 4
CW = KV // NJ
NH = 1
HW = KV // NH
MODE = ("y", "y", "y", "y")


def kernel(
    x_hbm, gain_ref, w_hbm, cot_hbm,
    val_ref, gw_ref, gt_ref,
    x_ref, cot_ref,
    w_all, normed, scale_b, sq_mine, sq_all,
    pv, r1, q2, r2, gs, s_mine, s_all,
    tf, tb, tr, t2, xs, xr, gsend, leaf, chain,
    wz_s, wz_r, wx_s, wx_r, sib_s, sib_r, sq_s, sq_r, st_s, st_r,
    r1_s, r1_r, r2_s, r2_r, a1_s, a1_r, a2_s, a2_r,
    core_s, core_r, xs_s, xs_r, leaf_s, leaf_r, chain_s, chain_r,
    in_sem,
):
    blk = lax.axis_index("blk")
    tp = lax.axis_index("tp")
    xlo = blk // (2 * NZ)
    z = (blk // 2) % NZ
    core = blk % 2
    xhi = tp // NY
    y = tp % NY
    sign = (1 - 2 * core, 2 * core - 1)

    def at_z(step, other_x=False):
        x = 1 - xlo if other_x else xlo
        return (x * (2 * NZ) + ((z + step + 2 * NZ) % NZ) * 2 + core, tp)

    sibling = (xlo * (2 * NZ) + z * 2 + 1 - core, tp)
    partner = at_z(0, True)

    def tp_peer(k):
        return (blk, (tp + k) % NT)

    def y_peer(k):
        return (blk, xhi * NY + (y + k) % NY)

    x_peer = (blk, (1 - xhi) * NY + y)

    def copy(src, dst, s, r, dev):
        return pltpu.make_async_remote_copy(
            src_ref=src, dst_ref=dst, send_sem=s, recv_sem=r, device_id=dev, device_id_type=MESH
        )

    sent = []

    def start(c):
        c.start()
        sent.append(c)

    def arrived(dst, r):
        copy(dst, dst, r, r, partner).wait_recv()

    def quarter(ref, q):
        return ref.at[pl.ds(q * 128, 128)]

    x_in = [
        pltpu.make_async_copy(quarter(x_hbm, q), quarter(x_ref, q), in_sem.at[q]) for q in range(4)
    ]
    w_in = pltpu.make_async_copy(w_hbm, w_all.at[xlo, z, core], in_sem.at[8])
    cot_in = [
        pltpu.make_async_copy(quarter(cot_hbm, q), quarter(cot_ref, q), in_sem.at[4 + q])
        for q in range(4)
    ]
    w_in.start()
    for c in x_in:
        c.start()

    barrier = pltpu.get_barrier_semaphore()
    peers = [partner, sibling]
    for step in (1, 2, -1, -2):
        peers += [at_z(step), at_z(step, True)]
    peers += [tp_peer(k) for k in range(1, NT)]
    for dev in peers:
        pl.semaphore_signal(barrier, inc=1, device_id=dev, device_id_type=MESH)

    for c in cot_in:
        c.start()
    for q in range(ROWS // 128):
        x_in[q].wait()
        rows = pl.ds(q * 128, 128)
        acc = jnp.zeros((128, 128), F32)
        for n in range(FEAT // 128):
            xf = x_ref[rows, n * 128 : (n + 1) * 128].astype(F32)
            acc += xf * xf
        sq_mine[:, rows] = jnp.sum(acc.T, axis=0, keepdims=True)
    w_in.wait()
    pl.semaphore_wait(barrier, len(peers))

    def origin(i, k):
        return (z - sign[i] * k + 2 * NZ) % NZ

    def w_block(h, i, k, other_x=False):
        x = 1 - xlo if other_x else xlo
        return w_all.at[x, origin(i, k), core, :, pl.ds(h * HW, HW)]

    def w_send(h, i, k, step, diag=False):
        b = w_block(h, i, k)
        r = wx_r if diag else wz_r
        s = wx_s if diag else wz_s
        start(copy(b, b, s.at[h, i, k + step], r.at[h, i, k + step], at_z(sign[i] * step, diag)))

    def w_cross(h, i, k):
        b = w_block(h, i, k)
        start(copy(b, b, wx_s.at[h, i, k], wx_r.at[h, i, k], partner))

    def w_wait(h, i, k):
        arrived(w_block(h, i, k), wz_r.at[h, i, k])

    def w_pair(h, i, k):
        arrived(w_block(h, i, k, True), wx_r.at[h, i, k])
        o = origin(i, k)
        b = w_all.at[:, o, core, :, pl.ds(h * HW, HW)]
        start(copy(b, b, sib_s.at[h, o], sib_r.at[h, o], sibling))

    def w_step(m):
        k = 2 * m
        for h in range(NH):
            for i in range(2):
                w_wait(h, i, k)
                if not (i == 1 and m == 3):
                    w_send(h, i, k, 2)
                    if m == 3:
                        w_send(h, i, k, 2, True)
                w_send(h, i, k, 1)
                if m == 3:
                    w_send(h, i, k, 1, True)
            for i in range(2):
                w_cross(h, i, k)
        for h in range(NH):
            for i in range(2):
                w_wait(h, i, k - 1)
                w_cross(h, i, k - 1)

    for h in range(NH):
        for step in (2, 1):
            for i in range(2):
                w_send(h, i, 0, step)
        w_cross(h, 0, 0)

    for k in range(1, NT):
        start(copy(sq_mine, sq_all.at[tp], sq_s.at[k], sq_r.at[NT - k], tp_peer(k)))
    sq_all[tp] = sq_mine[...]

    w_step(1)
    for h in range(NH):
        w_pair(h, 0, 0)

    for k in range(1, NT):
        arrived(sq_all.at[(tp + k) % NT], sq_r.at[k])
    total = sq_all[0]
    for k in range(1, NT):
        total = total + sq_all[k]
    scale_row = lax.rsqrt(total / D + EPS)
    for q in range(ROWS // 128):
        rows = pl.ds(q * 128, 128)
        sb = jnp.broadcast_to(scale_row[:, q * 128 : (q + 1) * 128], (128, 128)).T
        scale_b[rows, :] = sb

    @pl.loop(0, ROWS // 128)
    def _(q):
        rows = pl.ds(pl.multiple_of(q * 128, 128), 128)
        sb = scale_b[rows, :][:, :1]
        normed[rows, :] = (x_ref[rows, :].astype(F32) * sb * gain_ref[...]).astype(BF16)

    w_step(2)
    for h in range(NH):
        for k in (2, 1):
            for i in range(2):
                w_pair(h, i, k)

    for c in cot_in:
        c.wait()

    for q in range(4):
        part = lax.dot_general(
            normed[:, q * 256 : (q + 1) * 256], cot_ref[...], (((0,), (0,)), ((), ())),
            preferred_element_type=F32,
        )
        tf[q // 2, (q % 2) * 8 : (q % 2) * 8 + 8] = part.reshape(8, 2, 16, KV)

    @pl.loop(0, NZ)
    def _(n):
        for h in range(2):
            tb[h, n] = tf[h, n, 1 - core].astype(BF16)

    start(copy(tb, tr, core_s, core_r, sibling))

    w_step(3)
    for h in range(NH):
        for k in (4, 3):
            for i in range(2):
                w_pair(h, i, k)

    arrived(tr, core_r)

    order = [(0, 8)] + [(i, k) for k in (7, 6, 5, 4, 3, 2, 1) for i in range(2)] + [(0, 0)]
    for i, k in order:
        n = origin(i, k)
        xs[n] = (tf[1 - xlo, n, core] + tr[1 - xlo, n].astype(F32)).astype(BF16)
        start(copy(xs.at[n], xr.at[n], xs_s.at[n], xs_r.at[n], partner))

    @pl.loop(0, NZ)
    def _(n):
        t2[n] = tf[xlo, n, core] + tr[xlo, n].astype(F32)

    def w_finish(h):
        for k in (6, 5):
            for i in range(2):
                w_pair(h, i, k)
        for i, k in ((0, 7), (1, 7), (0, 8)):
            w_wait(h, i, k)
            w_pair(h, i, k)
        for o in range(NZ):
            arrived(w_all.at[:, o, 1 - core, :, pl.ds(h * HW, HW)], sib_r.at[h, o])

    def cols_of(j):
        return pl.ds(j * CW, CW)

    def partial(j):
        wc = w_all[:, :, :, :, j * CW : (j + 1) * CW].reshape(FEAT, CW)

        for h in range(2):
            p = jnp.dot(normed[h * 256 : (h + 1) * 256, :], wc, preferred_element_type=F32)
            pv[h, :, :, j * CW : (j + 1) * CW] = p.astype(BF16).reshape(NY, OWN, CW)

        if MODE[j] == "y":
            for k in (1, 3, 2):
                peer = (y + k) % NY
                start(copy(
                    pv.at[:, peer, :, cols_of(j)], r1.at[j, pl.ds(2 * (NY - k), 2)],
                    r1_s.at[j, k], r1_r.at[j, NY - k], y_peer(k),
                ))
        else:
            start(copy(
                pv.at[1 - xhi, :, :, cols_of(j)], r1.at[j, pl.ds(0, NY)],
                r1_s.at[j, 0], r1_r.at[j, 0], x_peer,
            ))

    def step_a(j):
        cols = slice(j * CW, (j + 1) * CW)
        if MODE[j] == "y":
            for k in range(1, NY):
                arrived(r1.at[j, pl.ds(2 * k, 2)], r1_r.at[j, k])
            for g in range(2):
                x = 1 - xhi if g == 0 else xhi
                acc = pv[x, y, :, cols].astype(F32)
                for k in range(1, NY):
                    acc += r1[j, 2 * k + x].astype(F32)
                if g == 0:
                    q2[j, 0] = acc.astype(BF16)
                    start(copy(q2.at[j, 0], r2.at[j, 0], r2_s.at[j, 0], r2_r.at[j, 0], x_peer))
                else:
                    s_part[j] = acc
        else:
            arrived(r1.at[j, pl.ds(0, NY)], r1_r.at[j, 0])
            for k in (1, 3, 2, 0):
                peer = (y + k) % NY
                acc = pv[xhi, peer, :, cols].astype(F32) + r1[j, peer].astype(F32)
                if k:
                    q2[j, k] = acc.astype(BF16)
                    start(copy(
                        q2.at[j, k], r2.at[j, NY - k], r2_s.at[j, k], r2_r.at[j, NY - k], y_peer(k)
                    ))
                else:
                    s_part[j] = acc

    s_part = {}
    s_sum = []

    def step_b(j):
        cols = slice(j * CW, (j + 1) * CW)
        v = s_part[j]
        for k in range(1, NY) if MODE[j] == "x" else (0,):
            arrived(r2.at[j, k], r2_r.at[j, k])
            v = v + r2[j, k].astype(F32)
        val_ref[xhi, y, :, cols] = v.astype(BF16)
        mine = val_ref.at[xhi, y, :, cols_of(j)]
        if MODE[j] == "y":
            start(copy(mine, mine, a1_s.at[j, 0], a1_r.at[j, 0], x_peer))
        else:
            for k in (1, 3, 2):
                start(copy(mine, mine, a1_s.at[j, k], a1_r.at[j, NY - k], y_peer(k)))
        prod = v * cot_ref[pl.ds(pl.multiple_of(tp * OWN, OWN), OWN), cols].astype(F32)
        for n in range(CW // 128):
            part = prod[:, n * 128 : (n + 1) * 128]
            s_sum.append(part)
        if len(s_sum) == NJ * CW // 128:
            acc = functools.reduce(lambda a, b: a + b, s_sum)
            wide = jnp.concatenate([acc, jnp.zeros((128 - OWN, 128), F32)], axis=0)
            s_mine[...] = jnp.sum(wide.T, axis=0, keepdims=True)
            for k in (1, 2, 3, 5, 6, 7, 4):
                start(copy(s_mine, s_all.at[tp], st_s.at[k], st_r.at[NT - k], tp_peer(k)))
            s_all[tp] = s_mine[...]

    def step_c(j):
        if MODE[j] == "y":
            theirs = val_ref.at[1 - xhi, y, :, cols_of(j)]
            arrived(theirs, a1_r.at[j, 0])
            both = val_ref.at[:, y, :, cols_of(j)]
            for k in (1, 3, 2):
                start(copy(both, both, a2_s.at[j, k], a2_r.at[j, NY - k], y_peer(k)))
        else:
            for k in range(1, NY):
                arrived(val_ref.at[xhi, (y + k) % NY, :, cols_of(j)], a1_r.at[j, k])
            four = val_ref.at[xhi, :, :, cols_of(j)]
            start(copy(four, four, a2_s.at[j, 0], a2_r.at[j, 0], x_peer))

    def step_d(j):
        if MODE[j] == "y":
            for k in range(1, NY):
                arrived(val_ref.at[:, (y + k) % NY, :, cols_of(j)], a2_r.at[j, k])
        else:
            arrived(val_ref.at[1 - xhi, :, :, cols_of(j)], a2_r.at[j, 0])

    def x_sum(i, k):
        n = origin(i, k)
        arrived(xr.at[n], xs_r.at[n])
        return t2[n] + xr[n].astype(F32)

    def g_leaf(k):
        m = (k - 1) // 2
        for i in range(2):
            gsend[i, k] = x_sum(i, k).astype(BF16)
            start(copy(gsend.at[i, k], leaf.at[i, m], leaf_s.at[i, m], leaf_r.at[i, m], at_z(-sign[i])))

    def g_chain(k):
        m = k // 2
        for i in range(2):
            if k == 8 and i == 1:
                continue
            acc = x_sum(i, k)
            if k < 8:
                arrived(leaf.at[i, m], leaf_r.at[i, m])
                acc += leaf[i, m].astype(F32)
                if not (i == 1 and m == 3):
                    arrived(chain.at[i, m], chain_r.at[i, m])
                    acc += chain[i, m].astype(F32)
            gsend[i, k] = acc.astype(BF16)
            start(copy(
                gsend.at[i, k], chain.at[i, m - 1], chain_s.at[i, m - 1], chain_r.at[i, m - 1],
                at_z(-2 * sign[i]),
            ))

    def g_last():
        acc = x_sum(0, 0)
        for i in range(2):
            arrived(leaf.at[i, 0], leaf_r.at[i, 0])
            arrived(chain.at[i, 0], chain_r.at[i, 0])
            acc += leaf[i, 0].astype(F32) + chain[i, 0].astype(F32)
        gw_ref[...] = acc

    def grad(q):
        cols = slice(q * 256, (q + 1) * 256)
        wq = w_all[q // 2, (q % 2) * 8 : (q % 2) * 8 + 8].reshape(256, KV)

        @pl.loop(0, 2)
        def _(h):
            rows = pl.ds(pl.multiple_of(h * 256, 256), 256)
            gn = lax.dot_general(
                cot_ref[rows, :], wq, (((1,), (1,)), ((), ())), preferred_element_type=F32
            )
            gs[rows, cols] = scale_b[rows, :][:, :1] * gain_ref[:, cols] * gn

    w_finish(0)
    partial(0)
    partial(1)
    partial(2)
    partial(3)
    g_chain(8)
    g_leaf(7)
    grad(0)
    step_a(0)
    g_leaf(5)
    step_a(1)
    g_chain(6)
    step_b(0)
    g_leaf(3)
    step_a(2)
    step_b(1)
    step_c(0)
    g_leaf(1)
    g_chain(4)
    step_a(3)
    step_b(2)
    step_c(1)
    grad(1)
    step_b(3)
    g_chain(2)
    step_c(2)
    grad(2)
    step_c(3)
    grad(3)

    for k in range(1, NT):
        arrived(s_all.at[(tp + k) % NT], st_r.at[k])
    for t in range(NT):
        rows = slice(t * OWN, (t + 1) * OWN)
        inner = jnp.broadcast_to(s_all[t], (128, 128)).T[:OWN]
        sb = scale_b[rows, :]
        coef = (sb * sb * inner / D)[:, :1]
        gt_ref[rows, :] = (gs[rows, :] - x_ref[rows, :].astype(F32) * coef).astype(BF16)
    g_last()
    for j in range(NJ):
        step_d(j)

    for c in sent:
        c.wait_send()


def hand_over(val_in, gw_in, gt_in, val_out, gw_out, gt_out, sem):
    copies = [pltpu.make_async_copy(gw_in, gw_out, sem.at[8])]
    for q in range(4):
        rows = pl.ds(q * 128, 128)
        copies.append(pltpu.make_async_copy(val_in.at[rows], val_out.at[rows], sem.at[q]))
        copies.append(pltpu.make_async_copy(gt_in.at[rows], gt_out.at[rows], sem.at[4 + q]))
    for c in copies:
        c.start()
    for c in copies:
        c.wait()


def on_device(tokens, gain, w_value, cotangent):
    vmem = pl.BlockSpec(memory_space=pltpu.VMEM)
    dma = pltpu.SemaphoreType.DMA
    hbm = pl.BlockSpec(memory_space=pl.ANY)
    scratch = [
        pltpu.VMEM((ROWS, FEAT), BF16),
        pltpu.VMEM((ROWS, KV), BF16),
        pltpu.VMEM((2, NZ, 2, 16, KV), BF16),
        pltpu.VMEM((ROWS, FEAT), BF16),
        pltpu.VMEM((ROWS, 128), F32),
        pltpu.VMEM((1, ROWS), F32),
        pltpu.VMEM((NT, 1, ROWS), F32),
        pltpu.VMEM((2, NY, OWN, KV), BF16),
        pltpu.VMEM((NJ, 2 * NY, OWN, CW), BF16),
        pltpu.VMEM((NJ, NY, OWN, CW), BF16),
        pltpu.VMEM((NJ, NY, OWN, CW), BF16),
        pltpu.VMEM((ROWS, FEAT), F32),
        pltpu.VMEM((1, 128), F32),
        pltpu.VMEM((NT, 1, 128), F32),
        pltpu.VMEM((2, NZ, 2, 16, KV), F32),
        pltpu.VMEM((2, NZ, 16, KV), BF16),
        pltpu.VMEM((2, NZ, 16, KV), BF16),
        pltpu.VMEM((NZ, 16, KV), F32),
        pltpu.VMEM((NZ, 16, KV), BF16),
        pltpu.VMEM((NZ, 16, KV), BF16),
        pltpu.VMEM((2, 9, 16, KV), BF16),
        pltpu.VMEM((2, 4, 16, KV), BF16),
        pltpu.VMEM((2, 4, 16, KV), BF16),
        dma((NH, 2, 9)), dma((NH, 2, 9)),
        dma((NH, 2, 9)), dma((NH, 2, 9)),
        dma((NH, NZ)), dma((NH, NZ)),
        dma((NT,)), dma((NT,)),
        dma((NT,)), dma((NT,)),
        dma((NJ, NY)), dma((NJ, NY)),
        dma((NJ, NY)), dma((NJ, NY)),
        dma((NJ, NY)), dma((NJ, NY)),
        dma((NJ, NY)), dma((NJ, NY)),
        dma, dma,
        dma((NZ,)), dma((NZ,)),
        dma((2, 4)), dma((2, 4)),
        dma((2, 4)), dma((2, 4)),
        dma((9,)),
    ]
    values, grad_weight, grad_tokens = pl.pallas_call(
        kernel,
        name="value_projection",
        out_shape=(
            pltpu.VMEM((2, NY, OWN, KV), BF16),
            pltpu.VMEM((16, KV), F32),
            pltpu.VMEM((ROWS, FEAT), BF16),
        ),
        in_specs=[hbm, vmem, hbm, hbm],
        out_specs=(vmem,) * 3,
        scratch_shapes=scratch,
        cost_estimate=pl.CostEstimate(
            flops=6 * ROWS * FEAT * KV, bytes_accessed=8 * 2**20, transcendentals=ROWS
        ),
        compiler_params=pltpu.CompilerParams(
            collective_id=0, has_side_effects=True, vmem_limit_bytes=56 * 2**20
        ),
    )(tokens, gain.reshape(1, FEAT), w_value, cotangent)
    return pl.pallas_call(
        hand_over,
        name="hand_over",
        out_shape=(
            jax.ShapeDtypeStruct((ROWS, KV), BF16),
            jax.ShapeDtypeStruct((16, KV), F32),
            jax.ShapeDtypeStruct((ROWS, FEAT), BF16),
        ),
        in_specs=[vmem] * 3,
        out_specs=(hbm,) * 3,
        scratch_shapes=[dma((9,))],
        compiler_params=pltpu.CompilerParams(vmem_limit_bytes=16 * 2**20),
    )(values.reshape(ROWS, KV), grad_weight, grad_tokens)


def solution(mesh):
    return jax.shard_map(
        on_device,
        mesh=mesh,
        in_specs=(P("blk", "tp"), P("tp"), P(("tp", "blk"), None), P("blk", None)),
        out_specs=(P("blk", None), P(("tp", "blk"), None), P("blk", "tp")),
        check_vma=False,
    )
```

time: 402 us -> 66.7 us (0.17)
  waiting for transfers between devices: 264 us -> 0 us
  blocking collectives: 107 us -> 0 us
  Pallas kernels: 0 us -> 65.3 us
  between operations: 14.1 us -> 0.64 us
  matrix products: 12.2 us -> 0 us
    reduce_scatter x1 -> x0, waiting for transfers between devices: 135 us -> none  [on_device(): grad_weight = lax.psum_scatter(term, 'blk', scatter_dimension=0, tiled=True)]
    all_gather x1 -> x0, waiting for transfers between devices: 128 us -> none  [on_device(): gathered = lax.all_gather(w_value, 'blk', axis=0, tiled=True)]
    psum x2 -> x0, blocking collectives: 107 us -> none  [the longest x1 84.1 us: on_device(): values = lax.psum(partial_value, 'tp').astype(jnp.bfloat16)]
    pallas_call x0 -> x2, Pallas kernels: none -> 65.3 us  [the longest x1 63.9 us: on_device(): pl.pallas_call(kernel, name='value_projection', out_shape=(pltpu.VMEM((2,...]
    dot_general x3 -> x0, matrix products: 12.2 us -> none  [the longest x1 4.57 us: on_device(): lax.dot_general(cotangent, gathered, (((1,), (1,)), ((), ())), preferred_...]
  transfers between devices with their start and end apart: 2 -> 0, of which waited for: 2 -> 0; matrix products, arithmetic and copies ran while one was open for 2% -> 0% of each run, Pallas kernels for 0% -> 0%
where the time goes in v2:
time: 66.7 us; the launch traced here: 65.9 us
  Pallas kernels  65.3 us (98%)
    pallas_call x1, Pallas kernels, on_device(): pl.pallas_call(kernel, name='value_projection', out_shape=(pltpu.VMEM((2,...  63.9 us
    pallas_call x1, Pallas kernels, on_device(): pl.pallas_call(hand_over, name='hand_over', out_shape=(jax.ShapeDtypeStru...  1.41 us

profile of v2, /device:TPU:6, one launch (start us, length us, event | category | flops | bytes accessed | tf_op | source)
XLA Modules:
  0.0 65.9 jit_solution(6815159734732669729)
XLA Ops:
  0.6 63.9 %value_projection.1 = (bf16[2,4,64,1024]{3,2,1,0:T(8,128)(2,1)S(1)}, f32[16,1024]{1,0:T(8,128)S(1)}, bf16[512,1024]{1,0:T(8,128)(2,1)S(1)}) custom-call(bf16[512,1024]{1,0:T(8,128)(2,1)} %x_hbm.1, f32[1,1024]{1,0:T(1,128)} %bitcast.3, bf16[16,1024]{1,0:T(8,128)(2,1)} %w_hbm.1, bf16[512,1024]{1,0:T(8,128)(2,1)} %cot_hbm.1), custom_call_target="tpu_custom_call" | custom-call | flops 3221225472 | bytes 8388608 | tf_op jit(solution)/shard_map/value_projection/pallas_call | solution.py:492
  64.5 1.4 %hand_over.1 = (bf16[512,1024]{1,0:T(8,128)(2,1)}, f32[16,1024]{1,0:T(8,128)}, bf16[512,1024]{1,0:T(8,128)(2,1)}) custom-call(bf16[512,1024]{1,0:T(8,128)(2,1)S(1)} %bitcast.2, f32[16,1024]{1,0:T(8,128)S(1)} %get-tuple-element.7.gw_in, bf16[512,1024]{1,0:T(8,128)(2,1)S(1)} %get-tuple-element.8.gt_in), custom_call_target="tpu_custom_call" | custom-call | tf_op jit(solution)/shard_map/hand_over/pallas_call | solution.py:510

commit v3 on v2

--- a/solution.py
+++ b/solution.py
@@ -24,13 +24,14 @@
 CW = KV // NJ
 NH = 1
 HW = KV // NH
-MODE = ("y", "y", "y", "y")
+SUM_FIRST = ("y", "y", "y", "y")
+SEND_LAST = ("y", "x", "y", "x")
 
 
 def kernel(
-    x_hbm, gain_ref, w_hbm, cot_hbm,
+    x_hbm, gain_hbm, w_hbm, cot_hbm,
     val_ref, gw_ref, gt_ref,
-    x_ref, cot_ref,
+    x_ref, cot_ref, gain_ref,
     w_all, normed, scale_b, sq_mine, sq_all,
     pv, r1, q2, r2, gs, s_mine, s_all,
     tf, tb, tr, t2, xs, xr, gsend, leaf, chain,
@@ -68,11 +69,8 @@
             src_ref=src, dst_ref=dst, send_sem=s, recv_sem=r, device_id=dev, device_id_type=MESH
         )
 
-    sent = []
-
     def start(c):
         c.start()
-        sent.append(c)
 
     def arrived(dst, r):
         copy(dst, dst, r, r, partner).wait_recv()
@@ -88,17 +86,73 @@
         pltpu.make_async_copy(quarter(cot_hbm, q), quarter(cot_ref, q), in_sem.at[4 + q])
         for q in range(4)
     ]
+    gain_in = pltpu.make_async_copy(gain_hbm, gain_ref, in_sem.at[9])
     w_in.start()
-    for c in x_in:
-        c.start()
 
     barrier = pltpu.get_barrier_semaphore()
     peers = [partner, sibling]
     for step in (1, 2, -1, -2):
         peers += [at_z(step), at_z(step, True)]
+    peers += [at_z(3), at_z(-3)]
     peers += [tp_peer(k) for k in range(1, NT)]
     for dev in peers:
         pl.semaphore_signal(barrier, inc=1, device_id=dev, device_id_type=MESH)
+    for c in x_in + [gain_in]:
+        c.start()
+
+    pl.semaphore_wait(barrier, len(peers))
+    w_in.wait()
+
+    def origin(i, k):
+        return (z - sign[i] * k + 2 * NZ) % NZ
+
+    def w_block(h, i, k, other_x=False):
+        x = 1 - xlo if other_x else xlo
+        return w_all.at[x, origin(i, k), core, :, pl.ds(h * HW, HW)]
+
+    def w_send(h, i, k, step, diag=False):
+        b = w_block(h, i, k)
+        r = wx_r if diag else wz_r
+        s = wz_s
+        start(copy(b, b, s.at[h], r.at[h, i, k + step], at_z(sign[i] * step, diag)))
+
+    def w_cross(h, i, k):
+        b = w_block(h, i, k)
+        start(copy(b, b, wx_s.at[h], wx_r.at[h, i, k], partner))
+
+    def w_wait(h, i, k):
+        arrived(w_block(h, i, k), wz_r.at[h, i, k])
+
+    def w_pair(h, i, k):
+        arrived(w_block(h, i, k, True), wx_r.at[h, i, k])
+        o = origin(i, k)
+        b = w_all.at[:, o, core, :, pl.ds(h * HW, HW)]
+        start(copy(b, b, sib_s.at[h], sib_r.at[h], sibling))
+
+    def w_step(k):
+        last = k == 6
+        for h in range(NH):
+            for i in range(2):
+                w_wait(h, i, k)
+                for step in (2, 1) if last else (3, 1, 2):
+                    if k + step == 8 and i == 1:
+                        continue
+                    w_send(h, i, k, step)
+                    if last:
+                        w_send(h, i, k, step, True)
+            for i in range(2):
+                w_cross(h, i, k)
+        for h in range(NH):
+            for near in (k - 2, k - 1):
+                for i in range(2):
+                    w_wait(h, i, near)
+                    w_cross(h, i, near)
+
+    for h in range(NH):
+        for step in (3, 1, 2):
+            for i in range(2):
+                w_send(h, i, 0, step)
+        w_cross(h, 0, 0)
 
     for c in cot_in:
         c.start()
@@ -110,70 +164,17 @@
             xf = x_ref[rows, n * 128 : (n + 1) * 128].astype(F32)
             acc += xf * xf
         sq_mine[:, rows] = jnp.sum(acc.T, axis=0, keepdims=True)
-    w_in.wait()
-    pl.semaphore_wait(barrier, len(peers))
-
-    def origin(i, k):
-        return (z - sign[i] * k + 2 * NZ) % NZ
-
-    def w_block(h, i, k, other_x=False):
-        x = 1 - xlo if other_x else xlo
-        return w_all.at[x, origin(i, k), core, :, pl.ds(h * HW, HW)]
-
-    def w_send(h, i, k, step, diag=False):
-        b = w_block(h, i, k)
-        r = wx_r if diag else wz_r
-        s = wx_s if diag else wz_s
-        start(copy(b, b, s.at[h, i, k + step], r.at[h, i, k + step], at_z(sign[i] * step, diag)))
-
-    def w_cross(h, i, k):
-        b = w_block(h, i, k)
-        start(copy(b, b, wx_s.at[h, i, k], wx_r.at[h, i, k], partner))
-
-    def w_wait(h, i, k):
-        arrived(w_block(h, i, k), wz_r.at[h, i, k])
-
-    def w_pair(h, i, k):
-        arrived(w_block(h, i, k, True), wx_r.at[h, i, k])
-        o = origin(i, k)
-        b = w_all.at[:, o, core, :, pl.ds(h * HW, HW)]
-        start(copy(b, b, sib_s.at[h, o], sib_r.at[h, o], sibling))
-
-    def w_step(m):
-        k = 2 * m
-        for h in range(NH):
-            for i in range(2):
-                w_wait(h, i, k)
-                if not (i == 1 and m == 3):
-                    w_send(h, i, k, 2)
-                    if m == 3:
-                        w_send(h, i, k, 2, True)
-                w_send(h, i, k, 1)
-                if m == 3:
-                    w_send(h, i, k, 1, True)
-            for i in range(2):
-                w_cross(h, i, k)
-        for h in range(NH):
-            for i in range(2):
-                w_wait(h, i, k - 1)
-                w_cross(h, i, k - 1)
-
-    for h in range(NH):
-        for step in (2, 1):
-            for i in range(2):
-                w_send(h, i, 0, step)
-        w_cross(h, 0, 0)
 
     for k in range(1, NT):
-        start(copy(sq_mine, sq_all.at[tp], sq_s.at[k], sq_r.at[NT - k], tp_peer(k)))
+        start(copy(sq_mine, sq_all.at[tp], sq_s, sq_r, tp_peer(k)))
     sq_all[tp] = sq_mine[...]
 
-    w_step(1)
+    w_step(3)
     for h in range(NH):
         w_pair(h, 0, 0)
 
-    for k in range(1, NT):
-        arrived(sq_all.at[(tp + k) % NT], sq_r.at[k])
+    gain_in.wait()
+    arrived(sq_all.at[pl.ds(0, NT - 1)], sq_r)
     total = sq_all[0]
     for k in range(1, NT):
         total = total + sq_all[k]
@@ -189,9 +190,9 @@
         sb = scale_b[rows, :][:, :1]
         normed[rows, :] = (x_ref[rows, :].astype(F32) * sb * gain_ref[...]).astype(BF16)
 
-    w_step(2)
+    w_step(6)
     for h in range(NH):
-        for k in (2, 1):
+        for k in (3, 1, 2):
             for i in range(2):
                 w_pair(h, i, k)
 
@@ -212,33 +213,26 @@
 
     start(copy(tb, tr, core_s, core_r, sibling))
 
-    w_step(3)
-    for h in range(NH):
-        for k in (4, 3):
-            for i in range(2):
-                w_pair(h, i, k)
-
     arrived(tr, core_r)
 
     order = [(0, 8)] + [(i, k) for k in (7, 6, 5, 4, 3, 2, 1) for i in range(2)] + [(0, 0)]
     for i, k in order:
         n = origin(i, k)
         xs[n] = (tf[1 - xlo, n, core] + tr[1 - xlo, n].astype(F32)).astype(BF16)
-        start(copy(xs.at[n], xr.at[n], xs_s.at[n], xs_r.at[n], partner))
+        start(copy(xs.at[n], xr.at[n], xs_s, xs_r.at[n], partner))
 
     @pl.loop(0, NZ)
     def _(n):
         t2[n] = tf[xlo, n, core] + tr[xlo, n].astype(F32)
 
     def w_finish(h):
-        for k in (6, 5):
+        for k in (6, 4, 5):
             for i in range(2):
                 w_pair(h, i, k)
         for i, k in ((0, 7), (1, 7), (0, 8)):
             w_wait(h, i, k)
             w_pair(h, i, k)
-        for o in range(NZ):
-            arrived(w_all.at[:, o, 1 - core, :, pl.ds(h * HW, HW)], sib_r.at[h, o])
+        arrived(w_all.at[:, :, 1 - core, :, pl.ds(h * HW, HW)], sib_r.at[h])
 
     def cols_of(j):
         return pl.ds(j * CW, CW)
@@ -250,24 +244,23 @@
             p = jnp.dot(normed[h * 256 : (h + 1) * 256, :], wc, preferred_element_type=F32)
             pv[h, :, :, j * CW : (j + 1) * CW] = p.astype(BF16).reshape(NY, OWN, CW)
 
-        if MODE[j] == "y":
+        if SUM_FIRST[j] == "y":
             for k in (1, 3, 2):
                 peer = (y + k) % NY
                 start(copy(
                     pv.at[:, peer, :, cols_of(j)], r1.at[j, pl.ds(2 * (NY - k), 2)],
-                    r1_s.at[j, k], r1_r.at[j, NY - k], y_peer(k),
+                    r1_s, r1_r.at[j], y_peer(k),
                 ))
         else:
             start(copy(
                 pv.at[1 - xhi, :, :, cols_of(j)], r1.at[j, pl.ds(0, NY)],
-                r1_s.at[j, 0], r1_r.at[j, 0], x_peer,
+                r1_s, r1_r.at[j], x_peer,
             ))
 
     def step_a(j):
         cols = slice(j * CW, (j + 1) * CW)
-        if MODE[j] == "y":
-            for k in range(1, NY):
-                arrived(r1.at[j, pl.ds(2 * k, 2)], r1_r.at[j, k])
+        if SUM_FIRST[j] == "y":
+            arrived(r1.at[j, pl.ds(2, 2 * NY - 2)], r1_r.at[j])
             for g in range(2):
                 x = 1 - xhi if g == 0 else xhi
                 acc = pv[x, y, :, cols].astype(F32)
@@ -275,18 +268,18 @@
                     acc += r1[j, 2 * k + x].astype(F32)
                 if g == 0:
                     q2[j, 0] = acc.astype(BF16)
-                    start(copy(q2.at[j, 0], r2.at[j, 0], r2_s.at[j, 0], r2_r.at[j, 0], x_peer))
+                    start(copy(q2.at[j, 0], r2.at[j, 0], r2_s, r2_r.at[j], x_peer))
                 else:
                     s_part[j] = acc
         else:
-            arrived(r1.at[j, pl.ds(0, NY)], r1_r.at[j, 0])
+            arrived(r1.at[j, pl.ds(0, NY)], r1_r.at[j])
             for k in (1, 3, 2, 0):
                 peer = (y + k) % NY
                 acc = pv[xhi, peer, :, cols].astype(F32) + r1[j, peer].astype(F32)
                 if k:
                     q2[j, k] = acc.astype(BF16)
                     start(copy(
-                        q2.at[j, k], r2.at[j, NY - k], r2_s.at[j, k], r2_r.at[j, NY - k], y_peer(k)
+                        q2.at[j, k], r2.at[j, NY - k], r2_s, r2_r.at[j], y_peer(k)
                     ))
                 else:
                     s_part[j] = acc
@@ -297,16 +290,17 @@
     def step_b(j):
         cols = slice(j * CW, (j + 1) * CW)
         v = s_part[j]
-        for k in range(1, NY) if MODE[j] == "x" else (0,):
-            arrived(r2.at[j, k], r2_r.at[j, k])
+        slots = (0, 1) if SUM_FIRST[j] == "y" else (1, NY)
+        arrived(r2.at[j, pl.ds(slots[0], slots[1] - slots[0])], r2_r.at[j])
+        for k in range(*slots):
             v = v + r2[j, k].astype(F32)
         val_ref[xhi, y, :, cols] = v.astype(BF16)
         mine = val_ref.at[xhi, y, :, cols_of(j)]
-        if MODE[j] == "y":
-            start(copy(mine, mine, a1_s.at[j, 0], a1_r.at[j, 0], x_peer))
+        if SEND_LAST[j] == "y":
+            start(copy(mine, mine, a1_s, a1_r.at[j], x_peer))
         else:
             for k in (1, 3, 2):
-                start(copy(mine, mine, a1_s.at[j, k], a1_r.at[j, NY - k], y_peer(k)))
+                start(copy(mine, mine, a1_s, a1_r.at[j], y_peer(k)))
         prod = v * cot_ref[pl.ds(pl.multiple_of(tp * OWN, OWN), OWN), cols].astype(F32)
         for n in range(CW // 128):
             part = prod[:, n * 128 : (n + 1) * 128]
@@ -316,28 +310,26 @@
             wide = jnp.concatenate([acc, jnp.zeros((128 - OWN, 128), F32)], axis=0)
             s_mine[...] = jnp.sum(wide.T, axis=0, keepdims=True)
             for k in (1, 2, 3, 5, 6, 7, 4):
-                start(copy(s_mine, s_all.at[tp], st_s.at[k], st_r.at[NT - k], tp_peer(k)))
+                start(copy(s_mine, s_all.at[tp], st_s, st_r, tp_peer(k)))
             s_all[tp] = s_mine[...]
 
     def step_c(j):
-        if MODE[j] == "y":
+        if SEND_LAST[j] == "y":
             theirs = val_ref.at[1 - xhi, y, :, cols_of(j)]
-            arrived(theirs, a1_r.at[j, 0])
+            arrived(theirs, a1_r.at[j])
             both = val_ref.at[:, y, :, cols_of(j)]
             for k in (1, 3, 2):
-                start(copy(both, both, a2_s.at[j, k], a2_r.at[j, NY - k], y_peer(k)))
+                start(copy(both, both, a2_s, a2_r.at[j], y_peer(k)))
         else:
-            for k in range(1, NY):
-                arrived(val_ref.at[xhi, (y + k) % NY, :, cols_of(j)], a1_r.at[j, k])
+            arrived(val_ref.at[0, pl.ds(0, NY - 1), :, cols_of(j)], a1_r.at[j])
             four = val_ref.at[xhi, :, :, cols_of(j)]
-            start(copy(four, four, a2_s.at[j, 0], a2_r.at[j, 0], x_peer))
+            start(copy(four, four, a2_s, a2_r.at[j], x_peer))
 
     def step_d(j):
-        if MODE[j] == "y":
-            for k in range(1, NY):
-                arrived(val_ref.at[:, (y + k) % NY, :, cols_of(j)], a2_r.at[j, k])
+        if SEND_LAST[j] == "y":
+            arrived(val_ref.at[:, pl.ds(0, NY - 1), :, cols_of(j)], a2_r.at[j])
         else:
-            arrived(val_ref.at[1 - xhi, :, :, cols_of(j)], a2_r.at[j, 0])
+            arrived(val_ref.at[1 - xhi, :, :, cols_of(j)], a2_r.at[j])
 
     def x_sum(i, k):
         n = origin(i, k)
@@ -348,7 +340,7 @@
         m = (k - 1) // 2
         for i in range(2):
             gsend[i, k] = x_sum(i, k).astype(BF16)
-            start(copy(gsend.at[i, k], leaf.at[i, m], leaf_s.at[i, m], leaf_r.at[i, m], at_z(-sign[i])))
+            start(copy(gsend.at[i, k], leaf.at[i, m], leaf_s, leaf_r.at[i, m], at_z(-sign[i])))
 
     def g_chain(k):
         m = k // 2
@@ -364,7 +356,7 @@
                     acc += chain[i, m].astype(F32)
             gsend[i, k] = acc.astype(BF16)
             start(copy(
-                gsend.at[i, k], chain.at[i, m - 1], chain_s.at[i, m - 1], chain_r.at[i, m - 1],
+                gsend.at[i, k], chain.at[i, m - 1], chain_s, chain_r.at[i, m - 1],
                 at_z(-2 * sign[i]),
             ))
 
@@ -418,8 +410,7 @@
     step_c(3)
     grad(3)
 
-    for k in range(1, NT):
-        arrived(s_all.at[(tp + k) % NT], st_r.at[k])
+    arrived(s_all.at[pl.ds(0, NT - 1)], st_r)
     for t in range(NT):
         rows = slice(t * OWN, (t + 1) * OWN)
         inner = jnp.broadcast_to(s_all[t], (128, 128)).T[:OWN]
@@ -430,8 +421,28 @@
     for j in range(NJ):
         step_d(j)
 
-    for c in sent:
-        c.wait_send()
+    def left(ref, s):
+        copy(ref, ref, s, s, partner).wait_send()
+
+    left(sq_all.at[pl.ds(0, NT - 1)], sq_s)
+    left(s_all.at[pl.ds(0, NT - 1)], st_s)
+    for h in range(NH):
+        part = pl.ds(h * HW, HW)
+        left(w_all.at[0, pl.ds(0, 9), :, :, part], wz_s.at[h])
+        left(w_all.at[0, pl.ds(0, 13), 0, :, part], wx_s.at[h])
+        left(w_all.at[:, :, 0, :, part], sib_s.at[h])
+    left(tb, core_s)
+    left(xs, xs_s)
+    left(leaf, leaf_s)
+    left(gsend.at[0, pl.ds(0, 7)], chain_s)
+    first = sum(6 if m == "y" else 4 for m in SUM_FIRST)
+    left(r1.at[:, pl.ds(0, first // NJ)], r1_s)
+    second = sum(1 if m == "y" else 3 for m in SUM_FIRST)
+    left(r1.at[:, pl.ds(0, second // NJ)], r2_s)
+    third = sum(1 if m == "y" else 3 for m in SEND_LAST)
+    left(r1.at[:, pl.ds(0, third // NJ)], a1_s)
+    fourth = sum(6 if m == "y" else 4 for m in SEND_LAST)
+    left(r1.at[:, pl.ds(0, fourth // NJ)], a2_s)
 
 
 def hand_over(val_in, gw_in, gt_in, val_out, gw_out, gt_out, sem):
@@ -453,6 +464,7 @@
     scratch = [
         pltpu.VMEM((ROWS, FEAT), BF16),
         pltpu.VMEM((ROWS, KV), BF16),
+        pltpu.VMEM((1, FEAT), F32),
         pltpu.VMEM((2, NZ, 2, 16, KV), BF16),
         pltpu.VMEM((ROWS, FEAT), BF16),
         pltpu.VMEM((ROWS, 128), F32),
@@ -474,20 +486,20 @@
         pltpu.VMEM((2, 9, 16, KV), BF16),
         pltpu.VMEM((2, 4, 16, KV), BF16),
         pltpu.VMEM((2, 4, 16, KV), BF16),
-        dma((NH, 2, 9)), dma((NH, 2, 9)),
-        dma((NH, 2, 9)), dma((NH, 2, 9)),
-        dma((NH, NZ)), dma((NH, NZ)),
-        dma((NT,)), dma((NT,)),
-        dma((NT,)), dma((NT,)),
-        dma((NJ, NY)), dma((NJ, NY)),
-        dma((NJ, NY)), dma((NJ, NY)),
-        dma((NJ, NY)), dma((NJ, NY)),
-        dma((NJ, NY)), dma((NJ, NY)),
+        dma((NH,)), dma((NH, 2, 9)),
+        dma((NH,)), dma((NH, 2, 9)),
+        dma((NH,)), dma((NH,)),
         dma, dma,
-        dma((NZ,)), dma((NZ,)),
-        dma((2, 4)), dma((2, 4)),
-        dma((2, 4)), dma((2, 4)),
-        dma((9,)),
+        dma, dma,
+        dma, dma((NJ,)),
+        dma, dma((NJ,)),
+        dma, dma((NJ,)),
+        dma, dma((NJ,)),
+        dma, dma,
+        dma, dma((NZ,)),
+        dma, dma((2, 4)),
+        dma, dma((2, 4)),
+        dma((10,)),
     ]
     values, grad_weight, grad_tokens = pl.pallas_call(
         kernel,
@@ -497,7 +509,7 @@
             pltpu.VMEM((16, KV), F32),
             pltpu.VMEM((ROWS, FEAT), BF16),
         ),
-        in_specs=[hbm, vmem, hbm, hbm],
+        in_specs=[hbm] * 4,
         out_specs=(vmem,) * 3,
         scratch_shapes=scratch,
         cost_estimate=pl.CostEstimate(

time: 66.7 us -> 63.8 us (0.957)
  Pallas kernels: 65.3 us -> 63 us
    pallas_call x1, Pallas kernels: 63.9 us -> 61.6 us  [on_device(): pl.pallas_call(kernel, name='value_projection', out_shape=(pltpu.VMEM((2,...]
where the time goes in v3:
time: 63.8 us; the launch traced here: 63.7 us
  Pallas kernels  63 us (99%)
  between operations  0.64 us (1%)
    pallas_call x1, Pallas kernels, on_device(): pl.pallas_call(kernel, name='value_projection', out_shape=(pltpu.VMEM((2,...  61.6 us
    pallas_call x1, Pallas kernels, on_device(): pl.pallas_call(hand_over, name='hand_over', out_shape=(jax.ShapeDtypeStru...  1.41 us

profile of v3, /device:TPU:6, one launch (start us, length us, event | category | flops | bytes accessed | tf_op | source)
XLA Modules:
  0.0 63.7 jit_solution(10939610315404039259)
XLA Ops:
  0.6 61.6 %value_projection.1 = (bf16[2,4,64,1024]{3,2,1,0:T(8,128)(2,1)S(1)}, f32[16,1024]{1,0:T(8,128)S(1)}, bf16[512,1024]{1,0:T(8,128)(2,1)S(1)}) custom-call(bf16[512,1024]{1,0:T(8,128)(2,1)} %x_hbm.1, f32[1,1024]{1,0:T(1,128)} %bitcast.3, bf16[16,1024]{1,0:T(8,128)(2,1)} %w_hbm.1, bf16[512,1024]{1,0:T(8,128)(2,1)} %cot_hbm.1), custom_call_target="tpu_custom_call" | custom-call | flops 3221225472 | bytes 8388608 | tf_op jit(solution)/shard_map/value_projection/pallas_call | solution.py:504
  62.3 1.4 %hand_over.1 = (bf16[512,1024]{1,0:T(8,128)(2,1)}, f32[16,1024]{1,0:T(8,128)}, bf16[512,1024]{1,0:T(8,128)(2,1)}) custom-call(bf16[512,1024]{1,0:T(8,128)(2,1)S(1)} %bitcast.2, f32[16,1024]{1,0:T(8,128)S(1)} %get-tuple-element.7.gw_in, bf16[512,1024]{1,0:T(8,128)(2,1)S(1)} %get-tuple-element.8.gt_in), custom_call_target="tpu_custom_call" | custom-call | tf_op jit(solution)/shard_map/hand_over/pallas_call | solution.py:522

commit v4 on v3

--- a/solution.py
+++ b/solution.py
@@ -191,35 +191,42 @@
         normed[rows, :] = (x_ref[rows, :].astype(F32) * sb * gain_ref[...]).astype(BF16)
 
     w_step(6)
+
+    def term(first):
+        x = 1 - xlo if first else xlo
+        for q in range(2):
+            cols = pl.ds(pl.multiple_of(x * (FEAT // 2) + q * 256, 256), 256)
+            part = lax.dot_general(
+                normed[:, cols], cot_ref[...], (((0,), (0,)), ((), ())), preferred_element_type=F32
+            )
+            tf[x, q * 8 : q * 8 + 8] = part.reshape(8, 2, 16, KV)
+
+        @pl.loop(0, NZ)
+        def _(n):
+            tb[x, n] = tf[x, n, 1 - core].astype(BF16)
+
+        slot = 0 if first else 1
+        start(copy(tb.at[x], tr.at[x], core_s.at[slot], core_r.at[slot], sibling))
+
+    for c in cot_in:
+        c.wait()
+    term(True)
+    term(False)
+
     for h in range(NH):
         for k in (3, 1, 2):
             for i in range(2):
                 w_pair(h, i, k)
 
-    for c in cot_in:
-        c.wait()
-
-    for q in range(4):
-        part = lax.dot_general(
-            normed[:, q * 256 : (q + 1) * 256], cot_ref[...], (((0,), (0,)), ((), ())),
-            preferred_element_type=F32,
-        )
-        tf[q // 2, (q % 2) * 8 : (q % 2) * 8 + 8] = part.reshape(8, 2, 16, KV)
-
-    @pl.loop(0, NZ)
-    def _(n):
-        for h in range(2):
-            tb[h, n] = tf[h, n, 1 - core].astype(BF16)
-
-    start(copy(tb, tr, core_s, core_r, sibling))
-
-    arrived(tr, core_r)
+    arrived(tr.at[1 - xlo], core_r.at[0])
 
     order = [(0, 8)] + [(i, k) for k in (7, 6, 5, 4, 3, 2, 1) for i in range(2)] + [(0, 0)]
     for i, k in order:
         n = origin(i, k)
         xs[n] = (tf[1 - xlo, n, core] + tr[1 - xlo, n].astype(F32)).astype(BF16)
         start(copy(xs.at[n], xr.at[n], xs_s, xs_r.at[n], partner))
+
+    arrived(tr.at[xlo], core_r.at[1])
 
     @pl.loop(0, NZ)
     def _(n):
@@ -388,26 +395,26 @@
     g_chain(8)
     g_leaf(7)
     grad(0)
+    grad(1)
     step_a(0)
-    g_leaf(5)
     step_a(1)
     g_chain(6)
+    g_leaf(5)
     step_b(0)
-    g_leaf(3)
     step_a(2)
     step_b(1)
     step_c(0)
-    g_leaf(1)
-    g_chain(4)
+    g_leaf(3)
     step_a(3)
     step_b(2)
     step_c(1)
-    grad(1)
+    g_chain(4)
+    g_leaf(1)
     step_b(3)
+    step_c(2)
     g_chain(2)
-    step_c(2)
+    step_c(3)
     grad(2)
-    step_c(3)
     grad(3)
 
     arrived(s_all.at[pl.ds(0, NT - 1)], st_r)
@@ -431,7 +438,8 @@
         left(w_all.at[0, pl.ds(0, 9), :, :, part], wz_s.at[h])
         left(w_all.at[0, pl.ds(0, 13), 0, :, part], wx_s.at[h])
         left(w_all.at[:, :, 0, :, part], sib_s.at[h])
-    left(tb, core_s)
+    left(tb.at[0], core_s.at[0])
+    left(tb.at[0], core_s.at[1])
     left(xs, xs_s)
     left(leaf, leaf_s)
     left(gsend.at[0, pl.ds(0, 7)], chain_s)
@@ -495,7 +503,7 @@
         dma, dma((NJ,)),
         dma, dma((NJ,)),
         dma, dma((NJ,)),
-        dma, dma,
+        dma((2,)), dma((2,)),
         dma, dma((NZ,)),
         dma, dma((2, 4)),
         dma, dma((2, 4)),

time: 63.8 us -> 63.4 us (level); the launches traced: 63.7 us -> 62.4 us
  Pallas kernels: 63 us -> 61.8 us
    pallas_call x1, Pallas kernels: 61.6 us -> 60.3 us  [on_device(): pl.pallas_call(kernel, name='value_projection', out_shape=(pltpu.VMEM((2,...]
where the time goes in v4:
time: 63.4 us; the launch traced here: 62.4 us
  Pallas kernels  61.8 us (97%)
  between operations  0.64 us (1%)
    pallas_call x1, Pallas kernels, on_device(): pl.pallas_call(kernel, name='value_projection', out_shape=(pltpu.VMEM((2,...  60.3 us
    pallas_call x1, Pallas kernels, on_device(): pl.pallas_call(hand_over, name='hand_over', out_shape=(jax.ShapeDtypeStru...  1.41 us

profile of v4, /device:TPU:6, one launch (start us, length us, event | category | flops | bytes accessed | tf_op | source)
XLA Modules:
  0.0 62.4 jit_solution(6418187661000066514)
XLA Ops:
  0.6 60.3 %value_projection.1 = (bf16[2,4,64,1024]{3,2,1,0:T(8,128)(2,1)S(1)}, f32[16,1024]{1,0:T(8,128)S(1)}, bf16[512,1024]{1,0:T(8,128)(2,1)S(1)}) custom-call(bf16[512,1024]{1,0:T(8,128)(2,1)} %x_hbm.1, f32[1,1024]{1,0:T(1,128)} %bitcast.3, bf16[16,1024]{1,0:T(8,128)(2,1)} %w_hbm.1, bf16[512,1024]{1,0:T(8,128)(2,1)} %cot_hbm.1), custom_call_target="tpu_custom_call" | custom-call | flops 3221225472 | bytes 8388608 | tf_op jit(solution)/shard_map/value_projection/pallas_call | solution.py:512
  61.0 1.4 %hand_over.1 = (bf16[512,1024]{1,0:T(8,128)(2,1)}, f32[16,1024]{1,0:T(8,128)}, bf16[512,1024]{1,0:T(8,128)(2,1)}) custom-call(bf16[512,1024]{1,0:T(8,128)(2,1)S(1)} %bitcast.2, f32[16,1024]{1,0:T(8,128)S(1)} %get-tuple-element.7.gw_in, bf16[512,1024]{1,0:T(8,128)(2,1)S(1)} %get-tuple-element.8.gt_in), custom_call_target="tpu_custom_call" | custom-call | tf_op jit(solution)/shard_map/hand_over/pallas_call | solution.py:530
